TPU v7x, 512 devices: a whole 4x8x8 slice. The times are simulated.
512 devices in a mesh: section: 32 (over z, x), leaf: 16 (over y, core).
Axes of the slice: x: 4, y: 8, z: 8, core: 2. Of those that a mesh axis runs over, the one named last changes fastest.
Arguments:
- query_feats: bfloat16 [65536, 300], P(('section', 'leaf')), may hold values from -6 to 6
- query_weight: float32 [65536], P('section'), may hold values from 0.02 to 0.2
- positive_label: int32 [65536, 8], P('section'), may hold values from 0 to 131071, as said below
- positive_bucket: int32 [65536, 8], P('section'), may hold values from 0 to 15
- inv_prop: float32 [16], replicated, may hold values from 1 to 10
- primary_w: bfloat16 [131072, 300], P(('section', 'leaf')), may hold values from -0.375 to 0.375
- copy_owner: int32 [131072], P(('section', 'leaf')), may hold values from 0 to 31, as said below
- copy_row: int32 [131072], P(('section', 'leaf')), may hold values from 0 to 255
Outputs:
- query_grad: float32 [65536, 300], P(('section', 'leaf'))
- primary_grad: float32 [131072, 300], P(('section', 'leaf'))
Inputs may be any that keep to these rules, and one draw needn't show every extreme that they name: `copy_owner`: each copy names a section other than its own device's; among the copies of one device at most 16 name one owner, and exactly 16 name one of them. `positive_label`: every listed label is the label of some slot, primary or copy, of the query's own section; a label may be listed twice.
All inputs are finite; a program needn't handle non-finite values.
Results may differ from a plain program's by a relative error of at most 0.0018.
Values may be sent and summed in bfloat16 or wider, within the bound.
No kernel may reach another device: no remote copies, remote signals or barrier semaphores. Data moves between devices by JAX's collectives and lax.ppermute only.
A program may use at most 64 MiB of HBM per device.

v0:
```python
import math
import jax
import jax.numpy as jnp
from jax import lax
from jax.sharding import PartitionSpec as P


def on_device(
    query_feats,
    query_weight,
    positive_label,
    positive_bucket,
    inv_prop,
    primary_w,
    copy_owner,
    copy_row,
):
    sections = lax.axis_size("section")
    leaves = lax.axis_size("leaf")
    section_id = lax.axis_index("section")
    leaf_id = lax.axis_index("leaf")
    prim_rows = primary_w.shape[0]
    copy_count = copy_owner.shape[0]
    feature_dim = primary_w.shape[1]
    capacity = 8 * ((2 * copy_count // (sections - 1) + 7) // 8)
    owner_hot = (copy_owner[:, None] == jnp.arange(sections, dtype=jnp.int32)[None, :]).astype(
        jnp.float32
    )
    before = jnp.cumsum(owner_hot, axis=0) - owner_hot
    rank_in = jnp.sum(before * owner_hot, axis=1).astype(jnp.int32)
    target = copy_owner * capacity + rank_in
    requests = (
        jnp.zeros((sections * capacity,), jnp.int32)
        .at[target]
        .set(copy_row)
        .reshape(sections, capacity)
    )
    wanted = lax.all_to_all(requests, "section", split_axis=0, concat_axis=0, tiled=True)
    served = jnp.take(primary_w, wanted.reshape(-1), axis=0).reshape(
        sections, capacity, feature_dim
    )
    arrived = lax.all_to_all(served, "section", split_axis=0, concat_axis=0, tiled=True)
    copy_w = jnp.take(arrived.reshape(sections * capacity, feature_dim), target, axis=0)
    weights = jnp.concatenate([primary_w, copy_w], axis=0)
    first_label = (section_id * leaves + leaf_id) * prim_rows
    labels = jnp.concatenate(
        [
            first_label + jnp.arange(prim_rows, dtype=jnp.int32),
            (copy_owner * leaves + leaf_id) * prim_rows + copy_row,
        ]
    )
    bucket_hot = positive_bucket[..., None] == jnp.arange(inv_prop.shape[0], dtype=jnp.int32)
    pos_value = jnp.sum(jnp.where(bucket_hot, inv_prop, 0.0), axis=-1)
    slot_count = weights.shape[0]
    section_rows = positive_label.shape[0]
    start_state = (
        jnp.zeros((slot_count, feature_dim), jnp.float32),
        jnp.zeros((section_rows, feature_dim), jnp.float32),
    )
    shard_rows = lax.all_gather(query_feats, "leaf", axis=0, tiled=True)
    piece_rows = shard_rows.shape[0]
    block_rows = math.gcd(piece_rows, 256)

    def block_step(block_num, partial_sums):
        slot_acc, query_acc = partial_sums
        offset_row = block_num * block_rows
        q_block = lax.dynamic_slice_in_dim(shard_rows, offset_row, block_rows, 0)
        labels_block = lax.dynamic_slice_in_dim(positive_label, offset_row, block_rows, 0)
        values_block = lax.dynamic_slice_in_dim(pos_value, offset_row, block_rows, 0)
        scale_block = lax.dynamic_slice_in_dim(query_weight, offset_row, block_rows, 0)
        logits = lax.dot_general(
            q_block, weights, (((1,), (1,)), ((), ())), preferred_element_type=jnp.float32
        )
        sigmoid_val = jax.nn.sigmoid(logits)
        hit_count = jnp.zeros(logits.shape, jnp.float32)
        pos_weight = jnp.zeros(logits.shape, jnp.float32)
        for column in range(labels_block.shape[1]):
            matched = (labels[None, :] == labels_block[:, column : column + 1]).astype(jnp.float32)
            hit_count = hit_count + matched
            pos_weight = pos_weight + matched * values_block[:, column : column + 1]
        mixed = (1.0 - jnp.minimum(hit_count, 1.0)) * sigmoid_val + pos_weight * (sigmoid_val - 1.0)
        coefficient = (scale_block[:, None] * mixed).astype(jnp.bfloat16)
        query_part = jnp.dot(coefficient, weights, preferred_element_type=jnp.float32)
        query_acc = lax.dynamic_update_slice_in_dim(query_acc, query_part, offset_row, 0)
        slot_acc = slot_acc + lax.dot_general(
            coefficient, q_block, (((0,), (0,)), ((), ())), preferred_element_type=jnp.float32
        )
        return (slot_acc, query_acc)

    slot_grad, query_sum = lax.fori_loop(0, piece_rows // block_rows, block_step, start_state)
    send_back = (
        jnp.zeros((sections * capacity, feature_dim), jnp.float32)
        .at[target]
        .set(slot_grad[prim_rows:])
        .reshape(sections, capacity, feature_dim)
    )
    returned = lax.all_to_all(send_back, "section", split_axis=0, concat_axis=0, tiled=True)
    primary_grad = (
        slot_grad[:prim_rows].at[wanted.reshape(-1)].add(returned.reshape(-1, feature_dim))
    )
    query_whole = lax.psum(query_sum, "leaf")
    query_grad = lax.dynamic_slice_in_dim(
        query_whole, leaf_id * query_feats.shape[0], query_feats.shape[0], 0
    )
    return (query_grad, primary_grad)


def solution(mesh):
    placed = (
        P(("section", "leaf"), None),
        P("section"),
        P("section", None),
        P("section", None),
        P(),
        P(("section", "leaf"), None),
        P(("section", "leaf")),
        P(("section", "leaf")),
    )
    return jax.shard_map(
        on_device,
        mesh=mesh,
        in_specs=placed,
        out_specs=(P(("section", "leaf"), None), P(("section", "leaf"), None)),
        check_vma=False,
    )
```

profile of v0, /device:TPU:1, one launch (start us, length us, event | category | flops | bytes accessed | tf_op | source)
XLA Modules:
  0.0 241.0 jit_solution(1173304423045071907)
XLA Ops:
  7.2 1.6 copy.31
  11.8 1.6 scatter_custom_fusion
  14.0 13.7 %all-to-all-start = ((s32[32,1,16]{2,1,0:T(1,128)}), s32[32,1,16]{2,1,0:T(1,128)S(1)}, u32[]{:S(2)}, u32[]{:S(2)}) async-start(s32[32,1,16]{2,1,0:T(1,128)} %bitcast.2), calls=%async_computation | async-start | bytes 32768 | tf_op jit(solution)/shard_map/all_to_all | solution.py:38
  27.8 1.1 copy.35
  28.9 7.4 %all-to-all-done = s32[32,1,16]{2,1,0:T(1,128)S(1)} async-done(((s32[32,1,16]{2,1,0:T(1,128)}), s32[32,1,16]{2,1,0:T(1,128)S(1)}, u32[]{:S(2)}, u32[]{:S(2)}) %all-to-all-start) | async-done | bytes 2080 | tf_op jit(solution)/shard_map/all_to_all | solution.py:38
  37.6 1.9 gather_fusion
  40.5 3.9 %all-to-all-start.1 = ((bf16[32,16,300]{2,1,0:T(8,128)(2,1)}), bf16[32,16,300]{2,1,0:T(8,128)(2,1)S(1)}, u32[]{:S(2)}, u32[]{:S(2)}) async-start(bf16[32,16,300]{2,1,0:T(8,128)(2,1)} %broadcast_select_fusion), calls=%async_computation.1 | async-start | bytes 786432 | tf_op jit(solution)/shard_map/all_to_all | solution.py:42
  45.4 10.8 %all-to-all-done.1 = bf16[32,16,300]{2,1,0:T(8,128)(2,1)S(1)} async-done(((bf16[32,16,300]{2,1,0:T(8,128)(2,1)}), bf16[32,16,300]{2,1,0:T(8,128)(2,1)S(1)}, u32[]{:S(2)}, u32[]{:S(2)}) %all-to-all-start.1) | async-done | bytes 307232 | tf_op jit(solution)/shard_map/all_to_all | solution.py:42
  56.3 1.2 gather_fusion.1
  58.3 51.9 %while.18 = (s32[]{:T(128)}, f32[512,300]{0,1:T(8,128)S(1)}, f32[2048,300]{0,1:T(8,128)S(1)}, f32[2048]{0:T(1024)}, s32[512]{0:T(512)S(1)}, /*index=5*/s32[2048,...) while((s32[]{:T(128)}, f32[512,300]{0,1:T(8,128)S(1)}, ...), condition=%wide.region_6.7_spmd.clone, body=%wide.region_5.6_spmd.clone.sunk | while | flops 242659344 | bytes 3474841 | solution.py:90
  59.1 1.1 constant_dynamic-slice_fusion.5
  60.2 1.1 constant_dynamic-slice_fusion.6
  61.3 2.0 fusion.53
  63.2 1.2 convolution_add_fusion.2
  65.6 1.1 constant_dynamic-slice_fusion.5
  66.7 1.1 constant_dynamic-slice_fusion.6
  67.8 2.0 fusion.53
  69.7 1.2 convolution_add_fusion.2
  72.1 1.1 constant_dynamic-slice_fusion.5
  73.1 1.1 constant_dynamic-slice_fusion.6
  74.2 2.0 fusion.53
  76.2 1.2 convolution_add_fusion.2
  78.6 1.1 constant_dynamic-slice_fusion.5
  79.6 1.1 constant_dynamic-slice_fusion.6
  80.7 2.0 fusion.53
  82.7 1.2 convolution_add_fusion.2
  85.0 1.1 constant_dynamic-slice_fusion.5
  86.1 1.1 constant_dynamic-slice_fusion.6
  87.2 2.0 fusion.53
  89.2 1.2 convolution_add_fusion.2
  91.5 1.1 constant_dynamic-slice_fusion.5
  92.6 1.1 constant_dynamic-slice_fusion.6
  93.7 2.0 fusion.53
  95.7 1.2 convolution_add_fusion.2
  98.0 1.1 constant_dynamic-slice_fusion.5
  99.1 1.1 constant_dynamic-slice_fusion.6
  100.2 2.0 fusion.53
  102.1 1.2 convolution_add_fusion.2
  105.6 1.1 constant_dynamic-slice_fusion.6
  106.7 2.0 fusion.53
  108.6 1.2 convolution_add_fusion.2
  110.2 1.4 copy-done
  111.9 2.3 scatter_custom_fusion.1
  114.2 10.0 %all-to-all-start.2 = ((f32[32,16,300]{2,1,0:T(8,128)}), f32[32,16,300]{2,1,0:T(8,128)S(1)}, u32[]{:S(2)}, u32[]{:S(2)}) async-start(f32[32,16,300]{2,1,0:T(8,128)} %bitcast.7), calls=%async_computation.2 | async-start | bytes 1572864 | tf_op jit(solution)/shard_map/all_to_all | solution.py:97
  124.5 21.2 %all-to-all-done.2 = f32[32,16,300]{2,1,0:T(8,128)S(1)} async-done(((f32[32,16,300]{2,1,0:T(8,128)}), f32[32,16,300]{2,1,0:T(8,128)S(1)}, u32[]{:S(2)}, u32[]{:S(2)}) %all-to-all-start.2) | async-done | bytes 614432 | tf_op jit(solution)/shard_map/all_to_all | solution.py:97
  145.7 3.8 %scatter_fusion = f32[256,300]{1,0:T(8,128)S(1)} fusion(f32[256,300]{1,0:T(8,128)S(1)} %slice.197, s32[512]{0:T(512)S(1)} %bitcast.110, f32[512,300]{1,0:T(8,128)S(1)} %bitcast.90), kind=kCustom, calls=%fused_computation.4 | custom fusion | flops 153600 | bytes 1845248 | tf_op jit(solution)/shard_map/scatter-add | solution.py:99
  150.3 82.2 %all-reduce.2.cloned.1.call-done = f32[2048,300]{0,1:T(8,128)} async-done(((f32[2048,300]{0,1:T(8,128)}), f32[2048,300]{0,1:T(8,128)}) %all-reduce.2.cloned.1.call-update) | async-done | bytes 2457616 | tf_op jit(solution)/shard_map/psum | solution.py:101
  232.5 1.6 constant_dynamic-slice_fusion.2
  (60 shorter events, 18.6 us)
Async XLA Ops:
  7.2 50.9 %all-gather.2.cloned.1.call-start = ((), (), s32[]{:S(2)}) async-start(), calls=%async_computation.3 | async-start | bytes 1671168 | tf_op jit(solution)/shard_map/all_gather | solution.py:60
  14.0 22.2 %all-to-all-start = ((s32[32,1,16]{2,1,0:T(1,128)}), s32[32,1,16]{2,1,0:T(1,128)S(1)}, u32[]{:S(2)}, u32[]{:S(2)}) async-start(s32[32,1,16]{2,1,0:T(1,128)} %bitcast.2), calls=%async_computation | async-start | bytes 32768 | tf_op jit(solution)/shard_map/all_to_all | solution.py:38
  37.6 6.9 %copy-start.2 = (s32[256]{0:T(256)S(1)}, s32[256]{0:T(256)}, u32[]{:S(2)}) copy-start(s32[256]{0:T(256)} %param.16) | copy-start | bytes 3076
  37.6 6.9 %copy-start.3 = (s32[256]{0:T(256)S(1)}, s32[256]{0:T(256)}, u32[]{:S(2)}) copy-start(s32[256]{0:T(256)} %param.17) | copy-start | bytes 3076
  37.6 6.9 %copy-start.1 = (s32[2048,8]{0,1:T(8,128)S(1)}, s32[2048,8]{0,1:T(8,128)}, u32[]{:S(2)}) copy-start(s32[2048,8]{0,1:T(8,128)} %param.13) | copy-start | bytes 196612
  37.6 6.9 %copy-start.4 = (f32[16]{0:T(128)S(1)}, f32[16]{0:T(128)}, u32[]{:S(2)}) copy-start(f32[16]{0:T(128)} %param.14) | copy-start | bytes 196
  40.5 15.8 %all-to-all-start.1 = ((bf16[32,16,300]{2,1,0:T(8,128)(2,1)}), bf16[32,16,300]{2,1,0:T(8,128)(2,1)S(1)}, u32[]{:S(2)}, u32[]{:S(2)}) async-start(bf16[32,16,300]{2,1,0:T(8,128)(2,1)} %broadcast_select_fusion), calls=%async_computation.1 | async-start | bytes 786432 | tf_op jit(solution)/shard_map/all_to_all | solution.py:42
  44.4 188.2 %all-reduce.2.cloned.1.call-start = ((), (), s32[]{:S(2)}) async-start(), calls=%async_computation.4 | async-start | bytes 4980736 | tf_op jit(solution)/shard_map/psum | solution.py:101
  110.2 1.5 copy-start
  114.2 31.5 %all-to-all-start.2 = ((f32[32,16,300]{2,1,0:T(8,128)}), f32[32,16,300]{2,1,0:T(8,128)S(1)}, u32[]{:S(2)}, u32[]{:S(2)}) async-start(f32[32,16,300]{2,1,0:T(8,128)} %bitcast.7), calls=%async_computation.2 | async-start | bytes 1572864 | tf_op jit(solution)/shard_map/all_to_all | solution.py:97
Sparse Core Ops, SparseCore 0:
  10.7 47.2 all-gather.1
  111.8 120.6 all-reduce.1
where the time goes:
time: 243 us; the launch traced here: 241 us
  waiting for transfers between devices  122 us (50%)
  local copies, waits for them, and re-layouts  39.2 us (16%)
  matrix products  28 us (12%)
  starting transfers between devices  27.7 us (11%)
  between operations  14.3 us (6%)
  other arithmetic  9.21 us (4%)
    psum x1, waiting for transfers between devices, on_device(): query_whole = lax.psum(query_sum, 'leaf')  82.2 us
    all_to_all x1, waiting for transfers between devices, on_device(): lax.all_to_all(send_back, 'section', split_axis=0, concat_axis=0, tiled=T...  21.2 us
    dot_general x8, matrix products, block_step(): lax.dot_general(q_block, weights, (((1,), (1,)), ((), ())), preferred_ele...  15.7 us
    all_to_all x1, starting transfers between devices, on_device(): lax.all_to_all(requests, 'section', split_axis=0, concat_axis=0, tiled=True)  13.7 us
    all_to_all x1, waiting for transfers between devices, on_device(): lax.all_to_all(served, 'section', split_axis=0, concat_axis=0, tiled=True)  10.8 us
    all_to_all x1, starting transfers between devices, on_device(): lax.all_to_all(send_back, 'section', split_axis=0, concat_axis=0, tiled=T...  10 us
    dot_general x8, matrix products, block_step(): lax.dot_general(coefficient, q_block, (((0,), (0,)), ((), ())), preferred...  10 us
    slice x8, local copies, waits for them, and re-layouts, block_step(): labels_block[:, column:column + 1]  8.72 us
  transfers between devices with their start and end apart: 5, of which 5 were waited for; matrix products, arithmetic and copies ran while one was open for 8% of the time, Pallas kernels for 0%

commit v1 on v0

--- a/solution.py
+++ b/solution.py
@@ -1,8 +1,16 @@
+import functools
 import math
 import jax
 import jax.numpy as jnp
 from jax import lax
 from jax.sharding import PartitionSpec as P
+
+
+def mark_screen(packet, lane_axis):
+    return lax.all_gather(packet, lane_axis).sum(axis=0)
+
+
+deliver_squares_up = functools.partial(mark_screen, lane_axis="leaf")
 
 
 def on_device(
@@ -98,7 +106,7 @@
     primary_grad = (
         slot_grad[:prim_rows].at[wanted.reshape(-1)].add(returned.reshape(-1, feature_dim))
     )
-    query_whole = lax.psum(query_sum, "leaf")
+    query_whole = deliver_squares_up(query_sum)
     query_grad = lax.dynamic_slice_in_dim(
         query_whole, leaf_id * query_feats.shape[0], query_feats.shape[0], 0
     )

time: 243 us -> 370 us (1.52)
  waiting for transfers between devices: 122 us -> 208 us
  local copies, waits for them, and re-layouts: 39.2 us -> 66.8 us
  other arithmetic: 9.21 us -> 17.1 us
  matrix products: 28 us -> 34 us
    all_gather x0 -> x1, waiting for transfers between devices: none -> 167 us  [mark_screen(): return lax.all_gather(packet, lane_axis).sum(axis=0)]
    psum x1 -> x0, waiting for transfers between devices: 82.2 us -> none  [on_device(): query_whole = lax.psum(query_sum, 'leaf')]
    unnamed x13 -> x12, local copies, waits for them, and re-layouts: 5.05 us -> 38.8 us
    reduce_sum x0 -> x1, other arithmetic: none -> 8.38 us  [mark_screen(): return lax.all_gather(packet, lane_axis).sum(axis=0)]
    slice x8, local copies, waits for them, and re-layouts: 8.56 us -> 0.75 us  [block_step(): pos_weight = pos_weight + matched * values_block[:, column:column + 1]]
    dot_general x8, matrix products: 2.36 us -> 8.47 us  [block_step(): jnp.dot(coefficient, weights, preferred_element_type=jnp.float32)]
  transfers between devices with their start and end apart: 5 -> 5, of which waited for: 5 -> 5; matrix products, arithmetic and copies ran while one was open for 8% -> 5% of each run, Pallas kernels for 0% -> 0%
where the time goes in v1:
time: 370 us; the launch traced here: 368 us
  waiting for transfers between devices  208 us (56%)
  local copies, waits for them, and re-layouts  66.8 us (18%)
  matrix products  34 us (9%)
  starting transfers between devices  27.7 us (7%)
  other arithmetic  17.1 us (5%)
  between operations  14.3 us (4%)
    all_gather x1, waiting for transfers between devices, mark_screen(): return lax.all_gather(packet, lane_axis).sum(axis=0)  167 us
    unnamed x12, local copies, waits for them, and re-layouts  38.8 us
    all_to_all x1, waiting for transfers between devices, on_device(): lax.all_to_all(send_back, 'section', split_axis=0, concat_axis=0, tiled=T...  21.2 us
    dot_general x8, matrix products, block_step(): lax.dot_general(q_block, weights, (((1,), (1,)), ((), ())), preferred_ele...  15.6 us
    all_to_all x1, starting transfers between devices, on_device(): lax.all_to_all(requests, 'section', split_axis=0, concat_axis=0, tiled=True)  13.7 us
    all_to_all x1, waiting for transfers between devices, on_device(): lax.all_to_all(served, 'section', split_axis=0, concat_axis=0, tiled=True)  11.5 us
    all_to_all x1, starting transfers between devices, on_device(): lax.all_to_all(send_back, 'section', split_axis=0, concat_axis=0, tiled=T...  10 us
    dot_general x8, matrix products, block_step(): lax.dot_general(coefficient, q_block, (((0,), (0,)), ((), ())), preferred...  9.94 us
  transfers between devices with their start and end apart: 5, of which 5 were waited for; matrix products, arithmetic and copies ran while one was open for 5% of the time, Pallas kernels for 0%

profile of v1, /device:TPU:1, one launch (start us, length us, event | category | flops | bytes accessed | tf_op | source)
XLA Modules:
  0.0 367.9 jit_solution(5609811879122531863)
XLA Ops:
  7.2 1.6 copy.31
  11.8 1.6 scatter_custom_fusion
  14.0 13.7 %all-to-all-start = ((s32[32,1,16]{2,1,0:T(1,128)}), s32[32,1,16]{2,1,0:T(1,128)S(1)}, u32[]{:S(2)}, u32[]{:S(2)}) async-start(s32[32,1,16]{2,1,0:T(1,128)} %bitcast.2), calls=%async_computation | async-start | bytes 32768 | tf_op jit(solution)/shard_map/all_to_all | solution.py:46
  27.8 1.1 copy.35
  28.9 7.4 %all-to-all-done = s32[32,1,16]{2,1,0:T(1,128)S(1)} async-done(((s32[32,1,16]{2,1,0:T(1,128)}), s32[32,1,16]{2,1,0:T(1,128)S(1)}, u32[]{:S(2)}, u32[]{:S(2)}) %all-to-all-start) | async-done | bytes 2080 | tf_op jit(solution)/shard_map/all_to_all | solution.py:46
  37.6 1.9 gather_fusion
  40.5 3.9 %all-to-all-start.1 = ((bf16[32,16,300]{2,1,0:T(8,128)(2,1)}), bf16[32,16,300]{2,1,0:T(8,128)(2,1)S(1)}, u32[]{:S(2)}, u32[]{:S(2)}) async-start(bf16[32,16,300]{2,1,0:T(8,128)(2,1)} %broadcast_select_fusion), calls=%async_computation.1 | async-start | bytes 786432 | tf_op jit(solution)/shard_map/all_to_all | solution.py:50
  44.8 11.5 %all-to-all-done.1 = bf16[32,16,300]{2,1,0:T(8,128)(2,1)S(1)} async-done(((bf16[32,16,300]{2,1,0:T(8,128)(2,1)}), bf16[32,16,300]{2,1,0:T(8,128)(2,1)S(1)}, u32[]{:S(2)}, u32[]{:S(2)}) %all-to-all-start.1) | async-done | bytes 307232 | tf_op jit(solution)/shard_map/all_to_all | solution.py:50
  56.3 1.2 gather_fusion.1
  58.0 1.8 broadcast_in_dim.53
  59.8 50.1 %while.18 = (s32[]{:T(128)}, f32[512,300]{0,1:T(8,128)S(1)}, f32[2048,300]{0,1:T(8,128)}, f32[2048]{0:T(1024)}, s32[512]{0:T(512)S(1)}, /*index=5*/s32[2048,8]{0...) while((s32[]{:T(128)}, f32[512,300]{0,1:T(8,128)S(1)}, ...), condition=%wide.region_6.7_spmd.clone, body=%wide.region_5.6_spmd.clone.sunk | while | flops 242659344 | bytes 3388817 | solution.py:98
  59.9 1.1 constant_dynamic-slice_fusion.6
  61.8 1.9 fusion.53
  63.7 1.1 convolution_dynamic-update-slice_fusion.2
  64.8 1.2 convolution_add_fusion.2
  66.1 1.1 constant_dynamic-slice_fusion.6
  68.0 1.9 fusion.53
  70.0 1.1 convolution_dynamic-update-slice_fusion.2
  71.0 1.2 convolution_add_fusion.2
  72.4 1.3 constant_dynamic-slice_fusion.6
  74.4 1.9 fusion.53
  76.4 1.1 convolution_dynamic-update-slice_fusion.2
  77.5 1.2 convolution_add_fusion.2
  78.8 1.1 constant_dynamic-slice_fusion.6
  80.7 1.9 fusion.53
  83.7 1.2 convolution_add_fusion.2
  85.1 1.1 constant_dynamic-slice_fusion.6
  86.9 1.9 fusion.53
  88.9 1.1 convolution_dynamic-update-slice_fusion.2
  89.9 1.2 convolution_add_fusion.2
  91.3 1.1 constant_dynamic-slice_fusion.6
  93.2 1.9 fusion.53
  96.1 1.2 convolution_add_fusion.2
  97.5 1.1 constant_dynamic-slice_fusion.6
  99.4 1.9 fusion.53
  102.3 1.2 convolution_add_fusion.2
  103.7 1.1 constant_dynamic-slice_fusion.6
  105.6 1.9 fusion.53
  107.5 1.1 convolution_dynamic-update-slice_fusion.2
  108.6 1.2 convolution_add_fusion.2
  110.1 2.3 scatter_custom_fusion.1
  112.4 10.0 %all-to-all-start.2 = ((f32[32,16,300]{2,1,0:T(8,128)}), f32[32,16,300]{2,1,0:T(8,128)S(1)}, u32[]{:S(2)}, u32[]{:S(2)}) async-start(f32[32,16,300]{2,1,0:T(8,128)} %bitcast.7), calls=%async_computation.2 | async-start | bytes 1572864 | tf_op jit(solution)/shard_map/all_to_all | solution.py:105
  122.7 21.2 %all-to-all-done.2 = f32[32,16,300]{2,1,0:T(8,128)S(1)} async-done(((f32[32,16,300]{2,1,0:T(8,128)}), f32[32,16,300]{2,1,0:T(8,128)S(1)}, u32[]{:S(2)}, u32[]{:S(2)}) %all-to-all-start.2) | async-done | bytes 614432 | tf_op jit(solution)/shard_map/all_to_all | solution.py:105
  143.9 3.9 %scatter_fusion = f32[256,300]{1,0:T(8,128)S(1)} fusion(f32[256,300]{1,0:T(8,128)S(1)} %slice.197, s32[512]{0:T(512)S(1)} %bitcast.116, f32[512,300]{1,0:T(8,128)S(1)} %bitcast.96), kind=kCustom, calls=%fused_computation.4 | custom fusion | flops 153600 | bytes 1845248 | tf_op jit(solution)/shard_map/scatter-add | solution.py:107
  148.7 167.1 %all-gather.6.cloned.1.call-done = f32[32768,300]{0,1:T(8,128)} async-done(((f32[2048,300]{0,1:T(8,128)}), f32[32768,300]{0,1:T(8,128)}) %all-gather.6.cloned.1.call-update) | async-done | bytes 39321616 | tf_op jit(solution)/shard_map/all_gather | solution.py:10
  315.9 35.2 %copy.40 = f32[38,8,16,2048]{3,2,1,0:T(8,128)S(1)} copy(f32[38,8,16,2048]{3,1,2,0:T(8,128)} %bitcast.94) | data formatting | bytes 79691776
  351.1 8.4 %bitcast_reduce_fusion = f32[2048,300]{0,1:T(8,128)} fusion(f32[304,16,2048]{2,1,0:T(8,128)S(1)} %bitcast.93), kind=kLoop, calls=%fused_computation.54 | loop fusion | flops 9216000 | bytes 41779200 | tf_op jit(solution)/shard_map/reduce_sum | solution.py:10
  359.5 1.6 constant_dynamic-slice_fusion.2
  (60 shorter events, 18.2 us)
Async XLA Ops:
  7.2 50.9 %all-gather.4.cloned.1.call-start = ((), (), s32[]{:S(2)}) async-start(), calls=%async_computation.3 | async-start | bytes 1671168 | tf_op jit(solution)/shard_map/all_gather | solution.py:68
  14.0 22.2 %all-to-all-start = ((s32[32,1,16]{2,1,0:T(1,128)}), s32[32,1,16]{2,1,0:T(1,128)S(1)}, u32[]{:S(2)}, u32[]{:S(2)}) async-start(s32[32,1,16]{2,1,0:T(1,128)} %bitcast.2), calls=%async_computation | async-start | bytes 32768 | tf_op jit(solution)/shard_map/all_to_all | solution.py:46
  37.6 6.9 %copy-start.1 = (s32[256]{0:T(256)S(1)}, s32[256]{0:T(256)}, u32[]{:S(2)}) copy-start(s32[256]{0:T(256)} %param.16) | copy-start | bytes 3076
  37.6 6.9 %copy-start.2 = (s32[256]{0:T(256)S(1)}, s32[256]{0:T(256)}, u32[]{:S(2)}) copy-start(s32[256]{0:T(256)} %param.17) | copy-start | bytes 3076
  37.6 6.9 %copy-start = (s32[2048,8]{0,1:T(8,128)S(1)}, s32[2048,8]{0,1:T(8,128)}, u32[]{:S(2)}) copy-start(s32[2048,8]{0,1:T(8,128)} %param.13) | copy-start | bytes 196612
  37.6 6.9 %copy-start.3 = (f32[16]{0:T(128)S(1)}, f32[16]{0:T(128)}, u32[]{:S(2)}) copy-start(f32[16]{0:T(128)} %param.14) | copy-start | bytes 196
  40.5 15.8 %all-to-all-start.1 = ((bf16[32,16,300]{2,1,0:T(8,128)(2,1)}), bf16[32,16,300]{2,1,0:T(8,128)(2,1)S(1)}, u32[]{:S(2)}, u32[]{:S(2)}) async-start(bf16[32,16,300]{2,1,0:T(8,128)(2,1)} %broadcast_select_fusion), calls=%async_computation.1 | async-start | bytes 786432 | tf_op jit(solution)/shard_map/all_to_all | solution.py:50
  44.4 271.5 %all-gather.6.cloned.1.call-start = ((), (), s32[]{:S(2)}) async-start(), calls=%async_computation.4 | async-start | bytes 42336256 | tf_op jit(solution)/shard_map/all_gather | solution.py:10
  112.4 31.5 %all-to-all-start.2 = ((f32[32,16,300]{2,1,0:T(8,128)}), f32[32,16,300]{2,1,0:T(8,128)S(1)}, u32[]{:S(2)}, u32[]{:S(2)}) async-start(f32[32,16,300]{2,1,0:T(8,128)} %bitcast.7), calls=%async_computation.2 | async-start | bytes 1572864 | tf_op jit(solution)/shard_map/all_to_all | solution.py:105
Sparse Core Ops, SparseCore 0:
  10.7 47.2 all-gather.3
  110.0 205.7 all-gather.5
